TPU v7x, 32 devices: a whole 2x2x4 slice. The times are simulated.
32 devices in a mesh: ia: 4 (over y, x), ja: 8 (over z, core).
Axes of the slice: x: 2, y: 2, z: 4, core: 2. Of those that a mesh axis runs over, the one named last changes fastest.
Arguments:
- phase_space: float32 [12, 8192], P(None, 'ja'), may hold values from -6 to 6
- star_mass: float32 [8192], P('ja'), may hold values from 6.1035156e-05 to 0.00024414062
- star_level: int32 [8192], P('ja'), may hold values from 0 to 3
- active_ids: int32 [2, 64, 128], P(None, 'ia'), may hold values from 0 to 8191, as said below
- active_counts: int32 [2, 64], P(None, 'ia'), may hold values from 1 to 128, as said below
Outputs:
- final_state: float32 [12, 8192], P(None, 'ja')
- active_force: float32 [2, 6, 8192], P(None, None, ('ia', 'ja'))
Inputs may be any that keep to these rules, and one draw needn't show every extreme that they name: `active_ids`: within one block step the 64 x 128 entries are distinct star numbers; entries of unused slots are ignored. `active_counts`: in every block step one block is full and one holds a single star.
All inputs are finite; a program needn't handle non-finite values.
Results may differ from a plain program's by a relative error of at most 0.00018.
Values sent between devices are 32-bit elements; how exact they have to be, the bound alone decides.
A program may use at most 64 MiB of HBM per device.

v0:
```python
import jax
import jax.numpy as jnp
from jax import lax
from jax.sharding import PartitionSpec as P

STEPS = 2
EPS2 = 0.01
STEP_TIME = 0.05


def predict(state, tau):
    tau_sq = tau * tau
    tau_cube = tau_sq * tau
    new_pos = (
        state[0:3] + state[3:6] * tau + state[6:9] * (tau_sq * 0.5) + state[9:12] * (tau_cube / 6.0)
    )
    new_vel = state[3:6] + state[6:9] * tau + state[9:12] * (tau_sq * 0.5)
    return (new_pos, new_vel)


def field_force(target_pos, target_vel, source_pos, source_vel, source_mass):
    offset = source_pos[:, None, :] - target_pos[:, :, None]
    rel_vel = source_vel[:, None, :] - target_vel[:, :, None]
    dist_sq = jnp.sum(offset * offset, axis=0) + EPS2
    inverse = lax.rsqrt(dist_sq)
    weight = source_mass[None, :] * inverse * inverse * inverse
    radial = 3.0 * jnp.sum(offset * rel_vel, axis=0) / dist_sq
    accel = jnp.sum(weight[None] * offset, axis=2)
    jolt = jnp.sum(weight[None] * (rel_vel - radial[None] * offset), axis=2)
    return jnp.concatenate([accel, jolt], axis=0)


def blocked_force(target_pos, target_vel, source_pos, source_vel, source_mass, block_rows):
    total_rows = target_pos.shape[1]
    block_count = total_rows // block_rows
    tiles = (
        target_pos.reshape(3, block_count, block_rows).transpose(1, 0, 2),
        target_vel.reshape(3, block_count, block_rows).transpose(1, 0, 2),
    )

    def one_tile(pair_tile):
        return field_force(pair_tile[0], pair_tile[1], source_pos, source_vel, source_mass)

    result = lax.map(one_tile, tiles)
    return result.transpose(1, 0, 2).reshape(6, total_rows)


def correct(active_rows, accel, jolt, span):
    half_step = span * 0.5
    twelfth = span * span / 12.0
    old_pos = active_rows[0:3]
    old_vel = active_rows[3:6]
    old_acc = active_rows[6:9]
    old_jerk = active_rows[9:12]
    new_vel = old_vel + (old_acc + accel) * half_step + (old_jerk - jolt) * twelfth
    new_pos = old_pos + (old_vel + new_vel) * half_step + (old_acc - accel) * twelfth
    return jnp.concatenate([new_pos, new_vel, accel, jolt], axis=0)


def local(phase_space, star_mass, star_level, active_ids, active_counts):
    shard_width = phase_space.shape[1]
    shard_start = lax.axis_index("ja") * shard_width
    block_rows = 512
    state = phase_space
    last = -STEP_TIME * star_level.astype(jnp.float32)
    force_steps = []
    for step_index in range(STEPS):
        clock = STEP_TIME * (step_index + 1)
        indices = active_ids[step_index].reshape(-1)
        slot_pos = lax.broadcasted_iota(jnp.int32, (active_ids.shape[1], active_ids.shape[2]), 1)
        usable = (slot_pos < active_counts[step_index][:, None]).reshape(-1)
        local_ids = indices - shard_start
        inside = (local_ids >= 0) & (local_ids < shard_width)
        clipped = jnp.clip(local_ids, 0, shard_width - 1)
        fpos, fvel = predict(state, clock - last)
        stacked = jnp.concatenate([state, last[None, :]], axis=0)
        picked = jnp.where(inside[None, :], jnp.take(stacked, clipped, axis=1), 0.0)
        target_state = lax.psum(picked, "ja")
        tpos, tvel = predict(target_state[0:12], clock - target_state[12])
        partial_value = blocked_force(tpos, tvel, fpos, fvel, star_mass, block_rows)
        write_ids = jnp.where(usable, indices, -1)
        forces = lax.psum(partial_value, "ja")
        share_len = forces.shape[1] // lax.axis_size("ja")
        share_start = lax.axis_index("ja") * share_len
        force_share = lax.dynamic_slice_in_dim(forces, share_start, share_len, 1)
        usable_share = lax.dynamic_slice_in_dim(usable, share_start, share_len, 0)
        force_steps.append(jnp.where(usable_share[None, :], force_share, 0.0))
        outgoing = correct(target_state[0:12], forces[0:3], forces[3:6], clock - target_state[12])
        returned, return_ids = (
            lax.all_gather(outgoing, "ia", axis=1, tiled=True),
            lax.all_gather(write_ids, "ia", axis=0, tiled=True),
        )
        placed_raw = return_ids - shard_start
        valid = (return_ids >= 0) & (placed_raw >= 0) & (placed_raw < shard_width)
        placed = jnp.where(valid, placed_raw, shard_width)
        state = state.at[:, placed].set(returned, mode="drop")
        last = last.at[placed].set(clock, mode="drop")
    return (state, jnp.stack(force_steps))


def solution(mesh):
    placed = (P(None, "ja"), P("ja"), P("ja"), P(None, "ia", None), P(None, "ia"))
    return jax.shard_map(
        local,
        mesh=mesh,
        in_specs=placed,
        out_specs=(P(None, "ja"), P(None, None, ("ia", "ja"))),
        check_vma=False,
    )
```

profile of v0, /device:TPU:0, one launch (start us, length us, event | category | flops | bytes accessed | tf_op | source)
XLA Modules:
  0.0 312.5 jit_solution(17012939076392843902)
XLA Ops:
  11.3 5.5 %gather_fusion = f32[2048,13]{1,0:T(8,128)S(1)} fusion(f32[13,1024]{0,1:T(8,128)S(1)} %copy.110, s32[2048]{0:T(1024)S(1)} %get-tuple-element.164), kind=kCustom, calls=%fused_computation.clone | custom fusion | bytes 221184 | tf_op jit(solution)/shard_map/jit(_take)/gather | solution.py:77
  17.9 9.6 %all_gather.14 = s32[8192]{0:T(1024)S(1)} all-gather(s32[2048]{0:T(1024)S(1)} %get-tuple-element.165), channel_id=1, replica_groups=mesh['ia'=4,'ja'=8] {'ia'}, dimensions={0}, use_global_device_ids=true | all-gather | bytes 40960 | tf_op jit(solution)/shard_map/all_gather | solution.py:91
  27.5 8.1 %all_gather.12 = s32[8192]{0:T(1024)S(1)} all-gather(s32[2048]{0:T(1024)S(1)} %get-tuple-element.166), channel_id=1, replica_groups=mesh['ia'=4,'ja'=8] {'ia'}, dimensions={0}, use_global_device_ids=true | all-gather | bytes 40960 | tf_op jit(solution)/shard_map/all_gather | solution.py:91
  35.7 30.4 %scatter_fusion.1 = f32[1024]{0:T(1024)S(1)} fusion(f32[1024]{0:T(1024)S(1)} %get-tuple-element.170, s32[8192]{0:T(1024)S(1)} %compare_select_fusion.1, f32[8192]{0:T(1024)S(1)} %broadcast.175), kind=kCustom, calls=%fused_computation.3 | custom fusion | bytes 131072 | tf_op jit(solution)/shard_map/scatter | solution.py:97
  66.9 7.9 %all-reduce.3.cloned.1.call-done = f32[13,2048]{1,0:T(8,128)} async-done(((f32[13,2048]{1,0:T(8,128)}), f32[13,2048]{1,0:T(8,128)}) %all-reduce.3.cloned.1.call-update) | async-done | bytes 106512 | tf_op jit(solution)/shard_map/psum | solution.py:78
  74.8 0.9 broadcast_multiply_fusion.1
  75.7 1.0 multiply_add_fusion.4
  76.8 20.9 %while.20 = (s32[]{:T(128)}, f32[4,6,512]{2,1,0:T(8,128)S(1)}, f32[1024]{0:T(1024)S(1)}, f32[3,1024]{1,0:T(4,128)S(1)}, f32[4,3,512]{2,1,0:T(4,128)S(1)}, /*inde...) while((s32[]{:T(128)}, f32[4,6,512]{2,1,0:T(8,128)S(1)}, f32[1024]{0:T(1024)S(1)}, ...), condition=%wide.region_6.8_spmd, body=%wide.region_1.7_spmd.sunk | while | flops 24117248 | bytes 16924772 | solution.py:44
  76.8 1.8 fusion.31
  78.6 0.9 multiply_divide_fusion.4
  79.5 2.4 fusion.32
  82.0 1.8 fusion.31
  83.8 0.9 multiply_divide_fusion.4
  84.8 2.4 fusion.32
  87.2 1.8 fusion.31
  89.0 0.9 multiply_divide_fusion.4
  90.0 2.4 fusion.32
  92.5 1.8 fusion.31
  94.3 0.9 multiply_divide_fusion.4
  95.2 2.4 fusion.32
  97.7 26.3 %psum.29 = f32[6,2048]{1,0:T(8,128)S(1)} all-reduce(f32[6,2048]{1,0:T(8,128)S(1)} %bitcast.106), channel_id=1, replica_groups=mesh['ia'=4,'ja'=8] {'ja'}, use_global_device_ids=true, to_apply=%region_7.9 | all-reduce | flops 12288 | bytes 98304 | tf_op jit(solution)/shard_map/psum | solution.py:82
  124.1 10.0 %all_gather.13 = f32[12,8192]{1,0:T(8,128)S(1)} all-gather(f32[12,2048]{1,0:T(8,128)S(1)} %pad_maximum_fusion.1), channel_id=1, replica_groups=mesh['ia'=4,'ja'=8] {'ia'}, dimensions={1}, use_global_device_ids=true | all-gather | bytes 491520 | tf_op jit(solution)/shard_map/all_gather | solution.py:90
  134.1 2.6 copy.115
  136.8 21.2 %scatter_fusion = f32[12,1024]{0,1:T(8,128)S(1)} fusion(f32[12,1024]{0,1:T(8,128)S(1)} %copy.114, s32[8192]{0:T(1024)S(1)} %compare_select_fusion.1, f32[8192,12]{1,0:T(8,128)} %copy.115), kind=kCustom, calls=%fused_computation.2 | custom fusion | bytes 1212416 | tf_op jit(solution)/shard_map/scatter | solution.py:96
  158.0 1.3 fusion.24
  159.5 7.6 %gather_fusion.1 = f32[2048,13]{1,0:T(8,128)} fusion(f32[13,1024]{0,1:T(8,128)S(1)} %pad_maximum_fusion, s32[2048]{0:T(1024)S(1)} %get-tuple-element.163), kind=kCustom, calls=%fused_computation.1.clone | custom fusion | bytes 221184 | tf_op jit(solution)/shard_map/jit(_take)/gather | solution.py:77
  167.1 1.6 copy.117
  169.3 1.2 copy.129
  171.2 50.0 %all-reduce.5.cloned.1.call-done = f32[13,2048]{1,0:T(8,128)} async-done(((f32[13,2048]{1,0:T(8,128)}), f32[13,2048]{1,0:T(8,128)}) %all-reduce.5.cloned.1.call-update) | async-done | bytes 106512 | tf_op jit(solution)/shard_map/psum | solution.py:78
  221.2 0.9 broadcast_multiply_fusion
  222.1 1.0 multiply_add_fusion.1
  223.1 20.9 %while.21 = (s32[]{:T(128)}, f32[4,6,512]{2,1,0:T(8,128)S(1)}, f32[1024]{0:T(1024)S(1)}, f32[3,1024]{1,0:T(4,128)S(1)}, f32[4,3,512]{2,1,0:T(4,128)S(1)}, /*inde...) while((s32[]{:T(128)}, f32[4,6,512]{2,1,0:T(8,128)S(1)}, f32[1024]{0:T(1024)S(1)}, ...), condition=%wide.region_16.18_spmd, body=%wide.region_11.17_spmd.sunk | while | flops 24117248 | bytes 16924772 | solution.py:44
  223.2 1.8 fusion.34
  225.0 0.9 multiply_divide_fusion.5
  225.9 2.4 fusion.35
  228.4 1.8 fusion.34
  230.2 0.9 multiply_divide_fusion.5
  231.2 2.4 fusion.35
  233.6 1.8 fusion.34
  235.4 0.9 multiply_divide_fusion.5
  236.4 2.4 fusion.35
  238.9 1.8 fusion.34
  240.7 0.9 multiply_divide_fusion.5
  241.6 2.4 fusion.35
  244.1 26.3 %psum.31 = f32[6,2048]{1,0:T(8,128)S(1)} all-reduce(f32[6,2048]{1,0:T(8,128)S(1)} %bitcast.105), channel_id=1, replica_groups=mesh['ia'=4,'ja'=8] {'ja'}, use_global_device_ids=true, to_apply=%region_17.19 | all-reduce | flops 12288 | bytes 98304 | tf_op jit(solution)/shard_map/psum | solution.py:82
  270.6 10.0 %all_gather.15 = f32[12,8192]{1,0:T(8,128)S(1)} all-gather(f32[12,2048]{1,0:T(8,128)S(1)} %pad_maximum_fusion.2), channel_id=1, replica_groups=mesh['ia'=4,'ja'=8] {'ia'}, dimensions={1}, use_global_device_ids=true | all-gather | bytes 491520 | tf_op jit(solution)/shard_map/all_gather | solution.py:90
  280.6 2.6 copy.124
  283.2 21.1 %scatter_fusion.2 = f32[12,1024]{0,1:T(8,128)S(1)} fusion(f32[12,1024]{0,1:T(8,128)S(1)} %scatter_fusion, s32[8192]{0:T(1024)S(1)} %compare_select_fusion, f32[8192,12]{1,0:T(8,128)} %copy.124), kind=kCustom, calls=%fused_computation.4 | custom fusion | bytes 1212416 | tf_op jit(solution)/shard_map/scatter | solution.py:96
  (65 shorter events, 9.3 us)
Async XLA Ops:
  7.2 67.6 %all-reduce.3.cloned.1.call-start = ((), (), s32[]{:S(2)}) async-start(), calls=%async_computation | async-start | bytes 262144 | tf_op jit(solution)/shard_map/psum | solution.py:78
  17.8 203.4 %all-reduce.5.cloned.1.call-start = ((), (), s32[]{:S(2)}) async-start(), calls=%async_computation.1 | async-start | bytes 262144 | tf_op jit(solution)/shard_map/psum | solution.py:78
  35.7 30.5 %copy-start = (f32[12,1024]{1,0:T(8,128)S(1)}, f32[12,1024]{1,0:T(8,128)}, u32[]{:S(2)}) copy-start(f32[12,1024]{1,0:T(8,128)} %param.11) | copy-start | bytes 147460
  35.7 41.0 %copy-start.3 = (f32[1024]{0:T(1024)S(1)}, f32[1024]{0:T(1024)}, u32[]{:S(2)}) copy-start(f32[1024]{0:T(1024)} %param.12) | copy-start | bytes 12292
  76.7 47.3 %copy-start.1 = (f32[13,2048]{1,0:T(8,128)S(1)}, f32[13,2048]{1,0:T(8,128)}, u32[]{:S(2)}) copy-start(f32[13,2048]{1,0:T(8,128)} %all-reduce.3.cloned.1.call-done) | copy-start | bytes 319492
  223.1 47.3 %copy-start.2 = (f32[13,2048]{1,0:T(8,128)S(1)}, f32[13,2048]{1,0:T(8,128)}, u32[]{:S(2)}) copy-start(f32[13,2048]{1,0:T(8,128)} %all-reduce.5.cloned.1.call-done) | copy-start | bytes 319492
Sparse Core Ops, SparseCore 0:
  17.9 56.8 all-reduce.2
  169.4 51.7 all-reduce.4
where the time goes:
time: 313 us
  local copies, waits for them, and re-layouts  98.5 us (31%)
  blocking collectives  90.4 us (29%)
  waiting for transfers between devices  57.9 us (18%)
  other arithmetic  50.9 us (16%)
  between operations  14.3 us (5%)
    psum x2, waiting for transfers between devices, local(): target_state = lax.psum(picked, 'ja')  57.9 us
    psum x2, blocking collectives, local(): forces = lax.psum(partial_value, 'ja')  52.7 us
    scatter x2, local copies, waits for them, and re-layouts, local(): state = state.at[:, placed].set(returned, mode='drop')  42.3 us
    scatter x1, local copies, waits for them, and re-layouts, local(): last = last.at[placed].set(clock, mode='drop')  30.4 us
    all_gather x2, blocking collectives, local(): lax.all_gather(outgoing, 'ia', axis=1, tiled=True)  20 us
    reduce_sum x8, other arithmetic, field_force(): accel = jnp.sum(weight[None] * offset, axis=2)  19.5 us
    all_gather x2, blocking collectives, local(): lax.all_gather(write_ids, 'ia', axis=0, tiled=True)  17.7 us
    gather x4, local copies, waits for them, and re-layouts, local(): picked = jnp.where(inside[None, :], jnp.take(stacked, clipped, axis=1), 0.0)  14.9 us
  transfers between devices with their start and end apart: 2, of which 2 were waited for; matrix products, arithmetic and copies ran while one was open for 11% of the time, Pallas kernels for 0%

commit v1 on v0

--- a/solution.py
+++ b/solution.py
@@ -79,7 +79,7 @@
         tpos, tvel = predict(target_state[0:12], clock - target_state[12])
         partial_value = blocked_force(tpos, tvel, fpos, fvel, star_mass, block_rows)
         write_ids = jnp.where(usable, indices, -1)
-        forces = lax.psum(partial_value, "ja")
+        forces = jnp.sum(jax.lax.all_gather(partial_value, "ja"), axis=0)
         share_len = forces.shape[1] // lax.axis_size("ja")
         share_start = lax.axis_index("ja") * share_len
         force_share = lax.dynamic_slice_in_dim(forces, share_start, share_len, 1)

time: 313 us -> 292 us (0.933)
  blocking collectives: 90.4 us -> 68.1 us
    psum x2 -> x0, blocking collectives: 52.7 us -> none  [local(): forces = lax.psum(partial_value, 'ja')]
    all_gather x0 -> x2, blocking collectives: none -> 29.7 us  [local(): forces = jnp.sum(jax.lax.all_gather(partial_value, 'ja'), axis=0)]
where the time goes in v1:
time: 292 us; the launch traced here: 291 us
  local copies, waits for them, and re-layouts  98.5 us (34%)
  blocking collectives  68.1 us (23%)
  waiting for transfers between devices  58.7 us (20%)
  other arithmetic  51 us (17%)
  between operations  14.3 us (5%)
    psum x2, waiting for transfers between devices, local(): target_state = lax.psum(picked, 'ja')  58.7 us
    scatter x2, local copies, waits for them, and re-layouts, local(): state = state.at[:, placed].set(returned, mode='drop')  42.3 us
    scatter x1, local copies, waits for them, and re-layouts, local(): last = last.at[placed].set(clock, mode='drop')  30.4 us
    all_gather x2, blocking collectives, local(): forces = jnp.sum(jax.lax.all_gather(partial_value, 'ja'), axis=0)  29.7 us
    all_gather x2, blocking collectives, local(): lax.all_gather(outgoing, 'ia', axis=1, tiled=True)  20.7 us
    reduce_sum x8, other arithmetic, field_force(): accel = jnp.sum(weight[None] * offset, axis=2)  19.5 us
    all_gather x2, blocking collectives, local(): lax.all_gather(write_ids, 'ia', axis=0, tiled=True)  17.7 us
    gather x4, local copies, waits for them, and re-layouts, local(): picked = jnp.where(inside[None, :], jnp.take(stacked, clipped, axis=1), 0.0)  14.9 us
  transfers between devices with their start and end apart: 2, of which 2 were waited for; matrix products, arithmetic and copies ran while one was open for 11% of the time, Pallas kernels for 0%

profile of v1, /device:TPU:0, one launch (start us, length us, event | category | flops | bytes accessed | tf_op | source)
XLA Modules:
  0.0 291.1 jit_solution(2669208929478808065)
XLA Ops:
  11.3 5.5 %gather_fusion = f32[2048,13]{1,0:T(8,128)S(1)} fusion(f32[13,1024]{0,1:T(8,128)S(1)} %copy.141, s32[2048]{0:T(1024)S(1)} %get-tuple-element.166), kind=kCustom, calls=%fused_computation.clone | custom fusion | bytes 221184 | tf_op jit(solution)/shard_map/jit(_take)/gather | solution.py:77
  17.9 9.6 %all_gather.21 = s32[8192]{0:T(1024)S(1)} all-gather(s32[2048]{0:T(1024)S(1)} %get-tuple-element.167), channel_id=1, replica_groups=mesh['ia'=4,'ja'=8] {'ia'}, dimensions={0}, use_global_device_ids=true | all-gather | bytes 40960 | tf_op jit(solution)/shard_map/all_gather | solution.py:91
  27.5 8.1 %all_gather.18 = s32[8192]{0:T(1024)S(1)} all-gather(s32[2048]{0:T(1024)S(1)} %get-tuple-element.168), channel_id=1, replica_groups=mesh['ia'=4,'ja'=8] {'ia'}, dimensions={0}, use_global_device_ids=true | all-gather | bytes 40960 | tf_op jit(solution)/shard_map/all_gather | solution.py:91
  35.7 30.4 %scatter_fusion.1 = f32[1024]{0:T(1024)S(1)} fusion(f32[1024]{0:T(1024)S(1)} %get-tuple-element.172, s32[8192]{0:T(1024)S(1)} %compare_select_fusion.1, f32[8192]{0:T(1024)S(1)} %broadcast.175), kind=kCustom, calls=%fused_computation.3 | custom fusion | bytes 131072 | tf_op jit(solution)/shard_map/scatter | solution.py:97
  66.9 7.9 %all-reduce.3.cloned.1.call-done = f32[13,2048]{1,0:T(8,128)} async-done(((f32[13,2048]{1,0:T(8,128)}), f32[13,2048]{1,0:T(8,128)}) %all-reduce.3.cloned.1.call-update) | async-done | bytes 106512 | tf_op jit(solution)/shard_map/psum | solution.py:78
  74.8 0.9 broadcast_multiply_fusion.1
  75.7 1.0 multiply_add_fusion.4
  76.8 20.9 %while.20 = (s32[]{:T(128)}, f32[4,6,512]{2,1,0:T(8,128)S(1)}, f32[1024]{0:T(1024)S(1)}, f32[3,1024]{1,0:T(4,128)S(1)}, f32[4,3,512]{2,1,0:T(4,128)S(1)}, /*inde...) while((s32[]{:T(128)}, f32[4,6,512]{2,1,0:T(8,128)S(1)}, f32[1024]{0:T(1024)S(1)}, ...), condition=%wide.region_6.8_spmd, body=%wide.region_1.7_spmd.sunk | while | flops 24117248 | bytes 16924772 | solution.py:44
  76.8 1.8 fusion.31
  78.6 0.9 multiply_divide_fusion.4
  79.5 2.4 fusion.32
  82.0 1.8 fusion.31
  83.8 0.9 multiply_divide_fusion.4
  84.8 2.4 fusion.32
  87.2 1.8 fusion.31
  89.0 0.9 multiply_divide_fusion.4
  90.0 2.4 fusion.32
  92.5 1.8 fusion.31
  94.3 0.9 multiply_divide_fusion.4
  95.2 2.4 fusion.32
  97.7 14.8 %all_gather.19 = f32[8,6,2048]{2,1,0:T(8,128)S(1)} all-gather(f32[1,6,2048]{2,1,0:T(8,128)S(1)} %bitcast.105), channel_id=1, replica_groups=mesh['ia'=4,'ja'=8] {'ja'}, dimensions={0}, use_global_device_ids=true | all-gather | bytes 442368 | tf_op jit(solution)/shard_map/all_gather | solution.py:82
  112.7 10.3 %all_gather.20 = f32[12,8192]{1,0:T(8,128)S(1)} all-gather(f32[12,2048]{1,0:T(8,128)S(1)} %pad_maximum_fusion.1), channel_id=1, replica_groups=mesh['ia'=4,'ja'=8] {'ia'}, dimensions={1}, use_global_device_ids=true | all-gather | bytes 491520 | tf_op jit(solution)/shard_map/all_gather | solution.py:90
  123.0 2.6 copy.146
  125.6 21.2 %scatter_fusion = f32[12,1024]{0,1:T(8,128)S(1)} fusion(f32[12,1024]{0,1:T(8,128)S(1)} %copy.145, s32[8192]{0:T(1024)S(1)} %compare_select_fusion.1, f32[8192,12]{1,0:T(8,128)} %copy.146), kind=kCustom, calls=%fused_computation.2 | custom fusion | bytes 1212416 | tf_op jit(solution)/shard_map/scatter | solution.py:96
  146.9 1.3 fusion.24
  148.4 7.6 %gather_fusion.1 = f32[2048,13]{1,0:T(8,128)} fusion(f32[13,1024]{0,1:T(8,128)S(1)} %pad_maximum_fusion, s32[2048]{0:T(1024)S(1)} %get-tuple-element.165), kind=kCustom, calls=%fused_computation.1.clone | custom fusion | bytes 221184 | tf_op jit(solution)/shard_map/jit(_take)/gather | solution.py:77
  155.9 1.6 copy.148
  158.2 1.2 copy.160
  160.1 50.8 %all-reduce.5.cloned.1.call-done = f32[13,2048]{1,0:T(8,128)} async-done(((f32[13,2048]{1,0:T(8,128)}), f32[13,2048]{1,0:T(8,128)}) %all-reduce.5.cloned.1.call-update) | async-done | bytes 106512 | tf_op jit(solution)/shard_map/psum | solution.py:78
  210.9 0.9 broadcast_multiply_fusion
  211.7 1.0 multiply_add_fusion.1
  212.8 20.9 %while.21 = (s32[]{:T(128)}, f32[4,6,512]{2,1,0:T(8,128)S(1)}, f32[1024]{0:T(1024)S(1)}, f32[3,1024]{1,0:T(4,128)S(1)}, f32[4,3,512]{2,1,0:T(4,128)S(1)}, /*inde...) while((s32[]{:T(128)}, f32[4,6,512]{2,1,0:T(8,128)S(1)}, f32[1024]{0:T(1024)S(1)}, ...), condition=%wide.region_16.18_spmd, body=%wide.region_11.17_spmd.sunk | while | flops 24117248 | bytes 16924772 | solution.py:44
  212.8 1.8 fusion.34
  214.6 0.9 multiply_divide_fusion.5
  215.6 2.4 fusion.35
  218.1 1.8 fusion.34
  219.9 0.9 multiply_divide_fusion.5
  220.8 2.4 fusion.35
  223.3 1.8 fusion.34
  225.1 0.9 multiply_divide_fusion.5
  226.0 2.4 fusion.35
  228.5 1.8 fusion.34
  230.3 0.9 multiply_divide_fusion.5
  231.3 2.4 fusion.35
  233.7 14.8 %all_gather.22 = f32[8,6,2048]{2,1,0:T(8,128)S(1)} all-gather(f32[1,6,2048]{2,1,0:T(8,128)S(1)} %bitcast.106), channel_id=1, replica_groups=mesh['ia'=4,'ja'=8] {'ja'}, dimensions={0}, use_global_device_ids=true | all-gather | bytes 442368 | tf_op jit(solution)/shard_map/all_gather | solution.py:82
  248.8 10.3 %all_gather.23 = f32[12,8192]{1,0:T(8,128)S(1)} all-gather(f32[12,2048]{1,0:T(8,128)S(1)} %pad_maximum_fusion.2), channel_id=1, replica_groups=mesh['ia'=4,'ja'=8] {'ia'}, dimensions={1}, use_global_device_ids=true | all-gather | bytes 491520 | tf_op jit(solution)/shard_map/all_gather | solution.py:90
  259.1 2.6 copy.155
  261.7 21.1 %scatter_fusion.2 = f32[12,1024]{0,1:T(8,128)S(1)} fusion(f32[12,1024]{0,1:T(8,128)S(1)} %scatter_fusion, s32[8192]{0:T(1024)S(1)} %compare_select_fusion, f32[8192,12]{1,0:T(8,128)} %copy.155), kind=kCustom, calls=%fused_computation.4 | custom fusion | bytes 1212416 | tf_op jit(solution)/shard_map/scatter | solution.py:96
  (67 shorter events, 9.4 us)
Async XLA Ops:
  7.2 67.6 %all-reduce.3.cloned.1.call-start = ((), (), s32[]{:S(2)}) async-start(), calls=%async_computation | async-start | bytes 262144 | tf_op jit(solution)/shard_map/psum | solution.py:78
  17.8 193.1 %all-reduce.5.cloned.1.call-start = ((), (), s32[]{:S(2)}) async-start(), calls=%async_computation.1 | async-start | bytes 262144 | tf_op jit(solution)/shard_map/psum | solution.py:78
  35.7 30.5 %copy-start = (f32[12,1024]{1,0:T(8,128)S(1)}, f32[12,1024]{1,0:T(8,128)}, u32[]{:S(2)}) copy-start(f32[12,1024]{1,0:T(8,128)} %param.11) | copy-start | bytes 147460
  35.7 41.0 %copy-start.3 = (f32[1024]{0:T(1024)S(1)}, f32[1024]{0:T(1024)}, u32[]{:S(2)}) copy-start(f32[1024]{0:T(1024)} %param.12) | copy-start | bytes 12292
  76.7 35.8 %copy-start.1 = (f32[13,2048]{1,0:T(8,128)S(1)}, f32[13,2048]{1,0:T(8,128)}, u32[]{:S(2)}) copy-start(f32[13,2048]{1,0:T(8,128)} %all-reduce.3.cloned.1.call-done) | copy-start | bytes 319492
  212.8 35.9 %copy-start.2 = (f32[13,2048]{1,0:T(8,128)S(1)}, f32[13,2048]{1,0:T(8,128)}, u32[]{:S(2)}) copy-start(f32[13,2048]{1,0:T(8,128)} %all-reduce.5.cloned.1.call-done) | copy-start | bytes 319492
Sparse Core Ops, SparseCore 0:
  17.9 56.8 all-reduce.2
  158.3 52.5 all-reduce.4
